TPU v7x, 32 devices: a whole 2x2x4 slice. The times are simulated.
32 devices in a mesh: row: 4 (over y, x), col: 8 (over z, core).
Axes of the slice: x: 2, y: 2, z: 4, core: 2. Of those that a mesh axis runs over, the one named last changes fastest.
Arguments:
- left_features: bfloat16 [384, 4096], P(('row', 'col')), may hold values from -6 to 6
- right_features: bfloat16 [384, 4096], P(('row', 'col')), may hold values from -6 to 6
- weight: bfloat16 [1024, 128], replicated, may hold values from -2 to 2
- bias: float32 [128], replicated, may hold values from -3 to 3
- upstream: bfloat16 [384, 384, 128], P('row', 'col'), may hold values from -0.59765625 to 0.59765625
Outputs:
- pair_out: bfloat16 [384, 384, 128], P('row', 'col')
- grad_left: bfloat16 [384, 4096], P(('row', 'col'))
- grad_right: bfloat16 [384, 4096], P(('row', 'col'))
- grad_weight: float32 [1024, 128], replicated
- grad_bias: float32 [128], replicated
All inputs are finite; a program needn't handle non-finite values.
Results may differ from a plain program's by a relative error of at most 0.0063.
Values may be sent and summed in bfloat16 or wider, within the bound.
A program may use at most 128 MiB of HBM per device.

v0:
```python
import jax
import jax.numpy as jnp
from jax import lax
from jax.sharding import PartitionSpec as P

CH = 32
SEQS = 128


block_rows = 16


def term_pass(row_feats, col_feats, weight, bias, grads, forms):
    count = row_feats.shape[0]
    across = col_feats.shape[0]
    width = row_feats.shape[1]
    pairs = weight.shape[1]
    scale = 1.0 / SEQS
    col3 = col_feats.reshape(across, SEQS, CH)
    weight_t = weight.T
    forward_form, row_form, col_form = forms

    def one_block(carry, index):
        d_cols, d_weight, d_bias = carry
        start = index * block_rows
        rows = lax.dynamic_slice_in_dim(row_feats, start, block_rows, 0).reshape(
            block_rows, SEQS, CH
        )
        outer = jnp.einsum(forward_form, rows, col3, preferred_element_type=jnp.float32) * scale
        outer = outer.reshape(block_rows * across, CH * CH).astype(jnp.bfloat16)
        pre = jnp.dot(outer, weight, preferred_element_type=jnp.float32) + bias
        active = jnp.maximum(pre, 0.0)
        squared = active * active
        grad_block = lax.dynamic_slice_in_dim(grads, start, block_rows, 0).reshape(
            block_rows * across, pairs
        )
        d_pre = (active * grad_block.astype(jnp.float32)).astype(jnp.bfloat16)
        d_outer = jnp.dot(d_pre, weight_t, preferred_element_type=jnp.float32).astype(jnp.bfloat16)
        d_outer = d_outer.reshape(block_rows, across, CH, CH)
        d_row = jnp.einsum(row_form, d_outer, col3, preferred_element_type=jnp.float32) * scale
        d_cols = (
            d_cols + jnp.einsum(col_form, d_outer, rows, preferred_element_type=jnp.float32) * scale
        )
        d_weight = d_weight + jnp.einsum(
            "pk,pe->ke", outer, d_pre, preferred_element_type=jnp.float32
        )
        d_bias = d_bias + jnp.sum(d_pre.astype(jnp.float32), axis=0)
        return (
            (d_cols, d_weight, d_bias),
            (squared.reshape(block_rows, across, pairs), d_row.reshape(block_rows, width)),
        )

    init = (
        jnp.zeros((across, SEQS, CH), jnp.float32),
        jnp.zeros((CH * CH, pairs), jnp.float32),
        jnp.zeros((pairs,), jnp.float32),
    )
    steps = count // block_rows
    (d_cols, d_weight, d_bias), (squared, d_rows) = lax.scan(
        one_block, init, jnp.arange(steps, dtype=jnp.int32)
    )
    return (
        squared.reshape(count, across, pairs),
        d_rows.reshape(count, width),
        d_cols.reshape(across, width),
        d_weight,
        d_bias,
    )


def local(left_features, right_features, weight, bias, upstream):
    ratio = lax.axis_size("col") // lax.axis_size("row")
    row_count = lax.axis_size("row")
    col_index = lax.axis_index("col")
    row_index = lax.axis_index("row")
    left_rows, right_rows = (
        lax.all_gather(left_features, "col", axis=0, tiled=True),
        lax.all_gather(right_features, "col", axis=0, tiled=True),
    )
    count = left_rows.shape[0]
    half = count // ratio
    part_rows = half // row_count
    portion = col_index % ratio
    owner = col_index // ratio
    left_piece = lax.dynamic_slice_in_dim(left_rows, portion * half, half, 0)
    right_piece = lax.dynamic_slice_in_dim(right_rows, portion * half, half, 0)
    left_recv, right_recv = (
        lax.all_to_all(left_piece, "row", split_axis=0, concat_axis=0, tiled=True),
        lax.all_to_all(right_piece, "row", split_axis=0, concat_axis=0, tiled=True),
    )
    left_part = lax.dynamic_slice_in_dim(left_recv, owner * part_rows, part_rows, 0)
    right_part = lax.dynamic_slice_in_dim(right_recv, owner * part_rows, part_rows, 0)
    left_cols, right_cols = (
        lax.all_gather(left_part, "row", axis=0, tiled=True),
        lax.all_gather(right_part, "row", axis=0, tiled=True),
    )
    direct_forms = ("isc,jsd->ijcd", "ijcd,jsd->isc", "ijcd,isc->jsd")
    mirror_forms = ("isd,jsc->ijcd", "ijcd,jsc->isd", "ijcd,isd->jsc")
    sq_direct, d_left_rows, d_right_cols, weight_one, bias_one = term_pass(
        left_rows, right_cols, weight, bias, upstream, direct_forms
    )
    sq_mirror, d_right_rows, d_left_cols, weight_two, bias_two = term_pass(
        right_rows, left_cols, weight, bias, upstream, mirror_forms
    )
    pair_out = ((sq_direct + sq_mirror) * 0.5).astype(jnp.bfloat16)
    left_total, right_total = lax.psum((d_left_cols, d_right_cols), "row")
    keep = (owner == row_index).astype(jnp.float32)
    start = portion * half
    left_slot = lax.dynamic_slice_in_dim(d_left_rows, start, half, 0) + keep * left_total
    right_slot = lax.dynamic_slice_in_dim(d_right_rows, start, half, 0) + keep * right_total
    d_left_rows = lax.dynamic_update_slice_in_dim(d_left_rows, left_slot, start, 0)
    d_right_rows = lax.dynamic_update_slice_in_dim(d_right_rows, right_slot, start, 0)
    grad_left, grad_right = (
        lax.psum_scatter(d_left_rows, "col", scatter_dimension=0, tiled=True),
        lax.psum_scatter(d_right_rows, "col", scatter_dimension=0, tiled=True),
    )
    grad_weight, grad_bias = lax.psum(
        (weight_one + weight_two, bias_one + bias_two), ("row", "col")
    )
    return (
        pair_out,
        grad_left.astype(jnp.bfloat16),
        grad_right.astype(jnp.bfloat16),
        grad_weight,
        grad_bias,
    )


def solution(mesh):
    placed = (P(("row", "col"), None), P(("row", "col"), None), P(), P(), P("row", "col", None))
    return jax.shard_map(
        local,
        mesh=mesh,
        in_specs=placed,
        out_specs=(
            P("row", "col", None),
            P(("row", "col"), None),
            P(("row", "col"), None),
            P(),
            P(),
        ),
        check_vma=False,
    )
```

profile of v0, /device:TPU:0, one launch (start us, length us, event | category | flops | bytes accessed | tf_op | source)
XLA Modules:
  0.0 870.2 jit_solution(4941487581606162873)
XLA Ops:
  7.2 18.6 %all-gather = bf16[8,12,4096]{2,1,0:T(8,128)(2,1)S(1)} all-gather(bf16[1,12,4096]{2,1,0:T(8,128)(2,1)} %bitcast.207), channel_id=1, replica_groups=mesh['row'=4,'col'=8] {'col'}, dimensions={0}, use_global_device_ids=true | all-gather | bytes 884736 | tf_op jit(solution)/shard_map/all_gather | solution.py:77
  32.7 17.3 %all-gather.1 = bf16[8,12,4096]{2,1,0:T(8,128)(2,1)S(1)} all-gather(bf16[1,12,4096]{2,1,0:T(8,128)(2,1)S(1)} %bitcast.208), channel_id=1, replica_groups=mesh['row'=4,'col'=8] {'col'}, dimensions={0}, use_global_device_ids=true | all-gather | bytes 884736 | tf_op jit(solution)/shard_map/all_gather | solution.py:78
  55.6 14.6 %all-gather.3 = bf16[4,12,4096]{2,1,0:T(8,128)(2,1)S(1)} all-gather(bf16[1,12,4096]{2,1,0:T(8,128)(2,1)S(1)} %dynamic-slice_bitcast_fusion), channel_id=1, replica_groups=mesh['row'=4,'col'=8] {'row'}, dimensions={0}, use_global_device_ids=true | all-gather | bytes 491520 | tf_op jit(solution)/shard_map/all_gather | solution.py:94
  75.7 286.7 %while.39 = (s32[]{:T(128)}, f32[48,128,32]{1,0,2:T(8,128)}, f32[1024,128]{1,0:T(8,128)}, f32[128]{0:T(128)S(1)}, f32[6,16,48,128]{3,2,1,0:T(8,128)}, /*index=5*...) while((s32[]{:T(128)}, f32[48,128,32]{1,0,2:T(8,128)}, ...), condition=%wide.region_5.6_spmd.clone, body=%wide.region_3.5_spmd.clone.sunk | while | flops 1212022912 | bytes 43782124 | solution.py:59
  81.4 6.8 copy.100
  88.2 6.1 convert_element_type.116
  100.8 6.0 reshape.117
  128.9 6.8 copy.100
  135.7 6.1 convert_element_type.116
  148.3 6.0 reshape.117
  164.7 5.2 fusion.128
  176.6 6.8 copy.100
  183.4 6.1 convert_element_type.116
  196.1 6.0 reshape.117
  212.5 5.2 fusion.128
  224.3 6.8 copy.100
  231.2 6.1 convert_element_type.116
  243.8 6.0 reshape.117
  272.0 6.8 copy.100
  278.8 6.1 convert_element_type.116
  291.5 6.0 reshape.117
  319.7 6.8 copy.100
  326.6 6.1 convert_element_type.116
  339.2 6.0 reshape.117
  370.4 9.2 %all-gather.2 = bf16[4,12,4096]{2,1,0:T(8,128)(2,1)S(1)} all-gather(bf16[1,12,4096]{2,1,0:T(8,128)(2,1)S(1)} %dynamic-slice_bitcast_fusion.1), channel_id=1, replica_groups=mesh['row'=4,'col'=8] {'row'}, dimensions={0}, use_global_device_ids=true | all-gather | bytes 491520 | tf_op jit(solution)/shard_map/all_gather | solution.py:95
  386.4 268.3 %while.38 = (s32[]{:T(128)}, f32[48,128,32]{1,0,2:T(8,128)}, f32[1024,128]{1,0:T(8,128)}, f32[128]{0:T(128)S(1)}, f32[6,16,48,128]{3,2,1,0:T(8,128)}, /*index=5*...) while((s32[]{:T(128)}, f32[48,128,32]{1,0,2:T(8,128)}, ...), condition=%wide.region_2.3_spmd.clone, body=%wide.region_0.2_spmd.clone.sunk | while | flops 1212022912 | bytes 47190044 | solution.py:59
  396.3 6.1 convert_element_type.112
  408.3 6.0 reshape.115
  422.2 7.1 fusion.112
  440.1 6.1 convert_element_type.112
  452.0 6.0 reshape.115
  467.0 7.1 fusion.112
  484.9 6.1 convert_element_type.112
  496.9 6.0 reshape.115
  511.9 7.1 fusion.112
  529.7 6.1 convert_element_type.112
  541.7 6.0 reshape.115
  556.7 7.1 fusion.112
  574.6 6.1 convert_element_type.112
  586.5 6.0 reshape.115
  601.5 7.1 fusion.112
  619.4 6.1 convert_element_type.112
  631.4 6.0 reshape.115
  646.4 7.1 fusion.112
  664.0 60.1 %all-reduce.11.cloned.1.call-done = (f32[48,4096]{1,0:T(8,128)}, f32[48,4096]{1,0:T(8,128)}) async-done(((f32[48,4096]{1,0:T(8,128)}, f32[48,4096]{1,0:T(8,128)}), (f32[48,4096]{1,0:T(8,128)}, f32[48,4096]{1,0:T(8,128)})) %all-reduce.11.cloned.1.call-update) | async-done | bytes 1572880 | tf_op jit(solution)/shard_map/psum | solution.py:106
  726.7 49.7 %fusion.50 = (f32[16,4096]{1,0:T(8,128)S(1)}, f32[16,4096]{1,0:T(8,128)S(1)}) fusion(f32[96,4096]{1,0:T(8,128)S(1)} %get-tuple-element.360, f32[96,4096]{1,0:T(8,128)} %get-tuple-element.359), kind=kCustom, calls=%all-reduce-scatter.2 | all-reduce-scatter fusion | flops 1048577 | bytes 3670528
  783.6 40.0 %psum.31 = f32[128]{0:T(128)} all-reduce(f32[128]{0:T(128)S(1)} %add.100), channel_id=1, replica_groups=mesh['row'=4,'col'=8] {'row','col'}, use_global_device_ids=true, to_apply=%region_11.12 | all-reduce | flops 128 | bytes 1024 | tf_op jit(solution)/shard_map/psum | solution.py:117
  832.8 28.4 %all-reduce.9.cloned.1.call-done = f32[1024,128]{1,0:T(8,128)} async-done(((f32[1024,128]{1,0:T(8,128)}), f32[1024,128]{1,0:T(8,128)}) %all-reduce.9.cloned.1.call-update) | async-done | bytes 524304 | tf_op jit(solution)/shard_map/psum | solution.py:117
  (507 shorter events, 367.4 us)
Async XLA Ops:
  28.8 21.4 %copy-start.7 = (bf16[1024,128]{1,0:T(8,128)(2,1)S(1)}, bf16[1024,128]{1,0:T(8,128)(2,1)}, u32[]{:S(2)}) copy-start(bf16[1024,128]{1,0:T(8,128)(2,1)} %param.11) | copy-start | bytes 786436
  28.8 22.5 %all-to-all-start.1 = ((bf16[4,12,4096]{2,1,0:T(8,128)(2,1)}), bf16[4,12,4096]{2,1,0:T(8,128)(2,1)S(1)}, u32[]{:S(2)}, u32[]{:S(2)}) async-start(bf16[4,12,4096]{2,1,0:T(8,128)(2,1)} %all_to_all.19), calls=%async_computation.1 | async-start | bytes 1048576 | tf_op jit(solution)/shard_map/all_to_all | solution.py:88
  51.3 317.9 %all-to-all-start = ((bf16[4,12,4096]{2,1,0:T(8,128)(2,1)}), bf16[4,12,4096]{2,1,0:T(8,128)(2,1)}, u32[]{:S(2)}, u32[]{:S(2)}) async-start(bf16[4,12,4096]{2,1,0:T(8,128)(2,1)} %all_to_all.16), calls=%async_computation | async-start | bytes 1048576 | tf_op jit(solution)/shard_map/all_to_all | solution.py:89
  55.4 668.6 %all-reduce.11.cloned.1.call-start = ((), (), s32[]{:S(2)}) async-start(), calls=%async_computation.3 | async-start | bytes 3145728 | tf_op jit(solution)/shard_map/psum | solution.py:106
  75.8 20.8 %copy-start.11 = (bf16[128,1024]{1,0:T(8,128)(2,1)}, bf16[128,1024]{1,0:T(8,128)(2,1)S(1)}, u32[]{:S(2)}) copy-start(bf16[128,1024]{1,0:T(8,128)(2,1)S(1)} %get-tuple-element.628) | copy-start | bytes 786436 | tf_op jit(solution)/shard_map/while
  123.3 20.8 %copy-start.11 = (bf16[128,1024]{1,0:T(8,128)(2,1)}, bf16[128,1024]{1,0:T(8,128)(2,1)S(1)}, u32[]{:S(2)}) copy-start(bf16[128,1024]{1,0:T(8,128)(2,1)S(1)} %get-tuple-element.628) | copy-start | bytes 786436 | tf_op jit(solution)/shard_map/while
  171.1 20.8 %copy-start.11 = (bf16[128,1024]{1,0:T(8,128)(2,1)}, bf16[128,1024]{1,0:T(8,128)(2,1)S(1)}, u32[]{:S(2)}) copy-start(bf16[128,1024]{1,0:T(8,128)(2,1)S(1)} %get-tuple-element.628) | copy-start | bytes 786436 | tf_op jit(solution)/shard_map/while
  218.8 20.8 %copy-start.11 = (bf16[128,1024]{1,0:T(8,128)(2,1)}, bf16[128,1024]{1,0:T(8,128)(2,1)S(1)}, u32[]{:S(2)}) copy-start(bf16[128,1024]{1,0:T(8,128)(2,1)S(1)} %get-tuple-element.628) | copy-start | bytes 786436 | tf_op jit(solution)/shard_map/while
  266.5 20.8 %copy-start.11 = (bf16[128,1024]{1,0:T(8,128)(2,1)}, bf16[128,1024]{1,0:T(8,128)(2,1)S(1)}, u32[]{:S(2)}) copy-start(bf16[128,1024]{1,0:T(8,128)(2,1)S(1)} %get-tuple-element.628) | copy-start | bytes 786436 | tf_op jit(solution)/shard_map/while
  314.2 20.8 %copy-start.11 = (bf16[128,1024]{1,0:T(8,128)(2,1)}, bf16[128,1024]{1,0:T(8,128)(2,1)S(1)}, u32[]{:S(2)}) copy-start(bf16[128,1024]{1,0:T(8,128)(2,1)S(1)} %get-tuple-element.628) | copy-start | bytes 786436 | tf_op jit(solution)/shard_map/while
  386.6 16.8 %copy-start.9 = (bf16[1024,128]{1,0:T(8,128)(2,1)}, bf16[1024,128]{1,0:T(8,128)(2,1)S(1)}, u32[]{:S(2)}) copy-start(bf16[1024,128]{1,0:T(8,128)(2,1)S(1)} %get-tuple-element.574) | copy-start | bytes 786436 | tf_op jit(solution)/shard_map/while
  386.6 18.2 %copy-start.13 = (bf16[128,1024]{1,0:T(8,128)(2,1)}, bf16[128,1024]{1,0:T(8,128)(2,1)S(1)}, u32[]{:S(2)}) copy-start(bf16[128,1024]{1,0:T(8,128)(2,1)S(1)} %get-tuple-element.577) | copy-start | bytes 786436 | tf_op jit(solution)/shard_map/while
  422.2 7.1 copy-start.6
  422.2 8.2 copy-start.10
  422.2 8.2 copy-start.14
  422.2 8.2 copy-start.18
  430.4 16.8 %copy-start.9 = (bf16[1024,128]{1,0:T(8,128)(2,1)}, bf16[1024,128]{1,0:T(8,128)(2,1)S(1)}, u32[]{:S(2)}) copy-start(bf16[1024,128]{1,0:T(8,128)(2,1)S(1)} %get-tuple-element.574) | copy-start | bytes 786436 | tf_op jit(solution)/shard_map/while
  430.4 18.2 %copy-start.13 = (bf16[128,1024]{1,0:T(8,128)(2,1)}, bf16[128,1024]{1,0:T(8,128)(2,1)S(1)}, u32[]{:S(2)}) copy-start(bf16[128,1024]{1,0:T(8,128)(2,1)S(1)} %get-tuple-element.577) | copy-start | bytes 786436 | tf_op jit(solution)/shard_map/while
  467.0 8.2 copy-start.10
  467.0 8.2 copy-start.14
  467.0 8.1 copy-start.18
  475.2 16.8 %copy-start.9 = (bf16[1024,128]{1,0:T(8,128)(2,1)}, bf16[1024,128]{1,0:T(8,128)(2,1)S(1)}, u32[]{:S(2)}) copy-start(bf16[1024,128]{1,0:T(8,128)(2,1)S(1)} %get-tuple-element.574) | copy-start | bytes 786436 | tf_op jit(solution)/shard_map/while
  475.2 18.2 %copy-start.13 = (bf16[128,1024]{1,0:T(8,128)(2,1)}, bf16[128,1024]{1,0:T(8,128)(2,1)S(1)}, u32[]{:S(2)}) copy-start(bf16[128,1024]{1,0:T(8,128)(2,1)S(1)} %get-tuple-element.577) | copy-start | bytes 786436 | tf_op jit(solution)/shard_map/while
  511.8 7.1 copy-start.6
  511.8 8.2 copy-start.10
  511.8 8.2 copy-start.14
  511.8 8.2 copy-start.18
  520.0 16.8 %copy-start.9 = (bf16[1024,128]{1,0:T(8,128)(2,1)}, bf16[1024,128]{1,0:T(8,128)(2,1)S(1)}, u32[]{:S(2)}) copy-start(bf16[1024,128]{1,0:T(8,128)(2,1)S(1)} %get-tuple-element.574) | copy-start | bytes 786436 | tf_op jit(solution)/shard_map/while
  520.0 18.2 %copy-start.13 = (bf16[128,1024]{1,0:T(8,128)(2,1)}, bf16[128,1024]{1,0:T(8,128)(2,1)S(1)}, u32[]{:S(2)}) copy-start(bf16[128,1024]{1,0:T(8,128)(2,1)S(1)} %get-tuple-element.577) | copy-start | bytes 786436 | tf_op jit(solution)/shard_map/while
  556.7 8.2 copy-start.10
  556.7 8.2 copy-start.14
  556.7 8.2 copy-start.18
  564.9 16.8 %copy-start.9 = (bf16[1024,128]{1,0:T(8,128)(2,1)}, bf16[1024,128]{1,0:T(8,128)(2,1)S(1)}, u32[]{:S(2)}) copy-start(bf16[1024,128]{1,0:T(8,128)(2,1)S(1)} %get-tuple-element.574) | copy-start | bytes 786436 | tf_op jit(solution)/shard_map/while
  564.9 18.2 %copy-start.13 = (bf16[128,1024]{1,0:T(8,128)(2,1)}, bf16[128,1024]{1,0:T(8,128)(2,1)S(1)}, u32[]{:S(2)}) copy-start(bf16[128,1024]{1,0:T(8,128)(2,1)S(1)} %get-tuple-element.577) | copy-start | bytes 786436 | tf_op jit(solution)/shard_map/while
  601.5 8.2 copy-start.10
  601.5 8.2 copy-start.14
  601.5 8.1 copy-start.18
  609.7 16.8 %copy-start.9 = (bf16[1024,128]{1,0:T(8,128)(2,1)}, bf16[1024,128]{1,0:T(8,128)(2,1)S(1)}, u32[]{:S(2)}) copy-start(bf16[1024,128]{1,0:T(8,128)(2,1)S(1)} %get-tuple-element.574) | copy-start | bytes 786436 | tf_op jit(solution)/shard_map/while
  609.7 18.2 %copy-start.13 = (bf16[128,1024]{1,0:T(8,128)(2,1)}, bf16[128,1024]{1,0:T(8,128)(2,1)S(1)}, u32[]{:S(2)}) copy-start(bf16[128,1024]{1,0:T(8,128)(2,1)S(1)} %get-tuple-element.577) | copy-start | bytes 786436 | tf_op jit(solution)/shard_map/while
  646.4 8.2 copy-start.10
  646.4 8.2 copy-start.14
  646.4 8.1 copy-start.18
  661.7 62.3 %copy-start.19 = (f32[6,16,4096]{2,1,0:T(8,128)S(1)}, f32[6,16,4096]{2,1,0:T(8,128)}, u32[]{:S(2)}) copy-start(f32[6,16,4096]{2,1,0:T(8,128)} %get-tuple-element.149) | copy-start | bytes 4718596
  661.8 199.5 %all-reduce.9.cloned.1.call-start = ((), (), s32[]{:S(2)}) async-start(), calls=%async_computation.2 | async-start | bytes 1048576 | tf_op jit(solution)/shard_map/psum | solution.py:117
  776.5 51.4 %collective-permute-start.2 = (bf16[16,4096]{1,0:T(8,128)(2,1)S(1)}, bf16[16,4096]{1,0:T(8,128)(2,1)S(1)}, u32[]{:S(2)}, u32[]{:S(2)}) collective-permute-start(bf16[16,4096]{1,0:T(8,128)(2,1)S(1)} %convert.23), channel_id=1, source_target_pairs={{0,1},{1,2},{2,3},{3,4},{4,5},{5,6},{6,7},{8,9},{9,10},{10,11},{11... | collective-permute-start | bytes 393224
  777.8 50.1 %collective-permute-start.3 = (bf16[12,4096]{1,0:T(8,128)(2,1)S(1)}, bf16[12,4096]{1,0:T(8,128)(2,1)S(1)}, u32[]{:S(2)}, u32[]{:S(2)}) collective-permute-start(bf16[12,4096]{1,0:T(8,128)(2,1)S(1)} %slice.1), channel_id=1, source_target_pairs={{0,2},{1,3},{2,4},{3,5},{4,6},{5,7},{8,10},{9,11},{10,12},{11,13},... | collective-permute-start | bytes 294920
  823.7 7.8 collective-permute-start
  825.6 5.9 collective-permute-start.1
  (88 other events, 334.4 us)
Sparse Core Ops, SparseCore 0:
  661.9 62.0 all-reduce.10
  730.7 130.4 all-reduce.8
where the time goes:
time: 877 us; the launch traced here: 870 us
  local copies, waits for them, and re-layouts  365 us (42%)
  matrix products  216 us (25%)
  blocking collectives  149 us (17%)
  waiting for transfers between devices  90.9 us (10%)
  starting transfers between devices  15.7 us (2%)
  between operations  15.2 us (2%)
  loops' own time  10.2 us (1%)
    convert_element_type x24, local copies, waits for them, and re-layouts, one_block(): outer = outer.reshape(block_rows * across, CH * CH).astype(jnp.bfloat16)  142 us
    dot_general x12, matrix products, one_block(): jnp.einsum(col_form, d_outer, rows, preferred_element_type=jnp.float32)  73.9 us
    reshape x12, local copies, waits for them, and re-layouts, one_block(): d_outer = d_outer.reshape(block_rows, across, CH, CH)  71.9 us
    psum x1, waiting for transfers between devices, local(): left_total, right_total = lax.psum((d_left_cols, d_right_cols), 'row')  60.1 us
    unnamed x1, blocking collectives  49.7 us
    dot_general x12, matrix products, one_block(): jnp.einsum(row_form, d_outer, col3, preferred_element_type=jnp.float32)  46.9 us
    psum x1, blocking collectives, local(): lax.psum((weight_one + weight_two, bias_one + bias_two), ('row', 'col'))  40 us
    dynamic_update_slice x24, local copies, waits for them, and re-layouts, term_pass(): lax.scan(one_block, init, jnp.arange(steps, dtype=jnp.int32))  30.6 us
  transfers between devices with their start and end apart: 8, of which 3 were waited for; matrix products, arithmetic and copies ran while one was open for 40% of the time, Pallas kernels for 0%

commit v1 on v0

v1 whole, which is shorter than its diff:
```python
import functools

import jax
import jax.numpy as jnp
from jax import lax
from jax.experimental import pallas as pl
from jax.experimental.pallas import tpu as pltpu
from jax.sharding import PartitionSpec as P

CH = 32
SEQS = 128
LANES = 128
F32 = jnp.float32
BF16 = jnp.bfloat16


def mm(a, b):
    return lax.dot_general(a, b, (((1,), (0,)), ((), ())), preferred_element_type=F32)


def mm_nt(a, b):
    return lax.dot_general(a, b, (((1,), (1,)), ((), ())), preferred_element_type=F32)


def tile_kernel(
    jb, ni, nj,
    rows_ref, cols_ref, wd_ref, wm_ref, wdt_ref, wmt_ref, bias_ref, up_ref,
    pair_ref, drows_ref, dcols_ref, dw_ref,
    rt, rx, bt, wide, x, gx, d, sq, u32, ut, drt, dw_m, dct, btt,
):
    step = pl.program_id(0)
    last = pl.num_programs(0) - 1
    pairs = wd_ref.shape[1]
    cc = CH * CH
    scale = 1.0 / SEQS
    ndev, _, part, _ = rows_ref.shape
    nparts = cols_ref.shape[0]
    pad = LANES - ni

    @pl.when(step == 0)
    def _():
        for side in range(2):
            for k in range(ndev):
                wide[pl.ds(k * part, part), :] = rows_ref[k, side].astype(F32)
            for k in range(nparts):
                bt[side, pl.ds(k * part, part), :] = cols_ref[k, side]

            def prep(c, _):
                block = wide[pl.ds(c, ni, stride=CH), :]
                if pad:
                    block = jnp.concatenate([block, jnp.zeros((pad, SEQS), F32)], axis=0)
                at = pl.multiple_of(c * LANES, LANES)
                rx[side, pl.ds(at, LANES), :] = block.astype(BF16)
                rt[side, :, pl.ds(at, LANES)] = block.T.astype(BF16)
                return 0

            lax.fori_loop(0, CH, prep, 0)
        drt[...] = jnp.zeros_like(drt)
        dw_ref[...] = jnp.zeros_like(dw_ref)
        dw_m[...] = jnp.zeros_like(dw_m)

    u32[...] = up_ref[...].astype(F32).reshape(ni * jb, pairs)
    for j in range(jb):
        block = u32[pl.ds(j, ni, stride=jb), :]
        if pad:
            block = jnp.concatenate([block, jnp.zeros((pad, pairs), F32)], axis=0)
        ut[:, j * LANES : (j + 1) * LANES] = block.T

    for side in range(2):
        w_ref, wt_ref = (wd_ref, wdt_ref) if side == 0 else (wm_ref, wmt_ref)
        base = pl.multiple_of(step * (jb * CH), jb * CH)
        bt_blk = bt[1 - side, pl.ds(base, jb * CH), :]
        btt[...] = bt_blk.astype(F32).T.astype(BF16)

        def first(cp, _):
            at = pl.multiple_of(cp * 2 * LANES, 2 * LANES)
            r = mm(bt[1 - side, pl.ds(base, jb * CH), :], rt[side, :, pl.ds(at, 2 * LANES)])
            r = (r * scale).astype(BF16)
            for c2 in range(2):
                to = pl.multiple_of(cp * 2 * CH + c2 * CH, CH)
                for j in range(jb):
                    x[pl.ds(to, CH), j * LANES : (j + 1) * LANES] = r[
                        j * CH : (j + 1) * CH, c2 * LANES : (c2 + 1) * LANES
                    ]
            return 0

        lax.fori_loop(0, CH // 2, first, 0)

        def second(jp, _):
            at = pl.multiple_of(jp * 2 * LANES, 2 * LANES)
            pre = mm(wt_ref[...], x[:, pl.ds(at, 2 * LANES)]) + bias_ref[...]
            active = jnp.maximum(pre, 0.0)
            d[:, pl.ds(at, 2 * LANES)] = (active * ut[:, pl.ds(at, 2 * LANES)]).astype(BF16)
            if side == 0:
                sq[:, pl.ds(at, 2 * LANES)] = active * active
            else:
                both = (sq[:, pl.ds(at, 2 * LANES)] + active * active) * 0.5
                flat = both.T
                for j2 in range(2):
                    u32[pl.ds(jp * 2 + j2, ni, stride=jb), :] = flat[j2 * LANES : j2 * LANES + ni]
            for m in range(cc // 256):
                g = mm(w_ref[m * 256 : (m + 1) * 256, :], d[:, pl.ds(at, 2 * LANES)]).astype(BF16)
                for c in range(256 // CH):
                    for j2 in range(2):
                        to = pl.multiple_of(jp * 2 * CH + j2 * CH, CH)
                        ch = m * (256 // CH) + c
                        gx[pl.ds(to, CH), ch * LANES : (ch + 1) * LANES] = g[
                            c * CH : (c + 1) * CH, j2 * LANES : (j2 + 1) * LANES
                        ]
            return 0

        lax.fori_loop(0, jb // 2, second, 0)

        def fourth(cp, _):
            at = pl.multiple_of(cp * 2 * LANES, 2 * LANES)
            drt[side, :, pl.ds(at, 2 * LANES)] += mm(btt[...], gx[:, pl.ds(at, 2 * LANES)])
            return 0

        lax.fori_loop(0, CH // 2, fourth, 0)

        def fifth(m, _):
            at = pl.multiple_of(m * 256, 256)
            dct[1 - side, pl.ds(pl.multiple_of(base + at, 256), 256), :] = (
                mm(gx[pl.ds(at, 256), :], rx[side]) * scale
            ).astype(BF16)
            return 0

        lax.fori_loop(0, jb * CH // 256, fifth, 0)

        target = dw_ref if side == 0 else dw_m

        def sixth(m, _):
            at = pl.multiple_of(m * 256, 256)
            target[pl.ds(at, 256), :] += mm_nt(x[pl.ds(at, 256), :], d[...])
            return 0

        lax.fori_loop(0, cc // 256, sixth, 0)
        dw_ref[cc : cc + 8, :] += mm_nt(jnp.ones((8, jb * LANES), BF16), d[...])

    pair_ref[...] = u32[...].reshape(ni, jb, pairs).astype(BF16)

    @pl.when(step == last)
    def _():
        for side in range(2):

            def unpack(c, _):
                at = pl.multiple_of(c * LANES, LANES)
                wide[pl.ds(c, ni, stride=CH), :] = drt[side, :, pl.ds(at, LANES)].T[:ni] * scale
                return 0

            lax.fori_loop(0, CH, unpack, 0)
            for k in range(ndev):
                drows_ref[k, side] = wide[pl.ds(k * part, part), :].astype(BF16)
            for k in range(nparts):
                dcols_ref[k, side] = dct[side, pl.ds(k * part, part), :]

        def merge(c, _):
            at = pl.multiple_of(c * CH, CH)
            dw_ref[pl.ds(at, CH), :] += dw_m[pl.ds(c, CH, stride=CH), :]
            return 0

        lax.fori_loop(0, CH, merge, 0)


def tile(rows, cols, weight, bias, upstream):
    ni, nj, pairs = upstream.shape
    jb = 16
    cc = CH * CH
    mirrored = weight.reshape(CH, CH, pairs).transpose(1, 0, 2).reshape(cc, pairs)
    whole = pl.BlockSpec(memory_space=pltpu.VMEM)
    fixed = lambda shape: pl.BlockSpec(shape, lambda g: (0,) * len(shape))
    return pl.pallas_call(
        functools.partial(tile_kernel, jb, ni, nj),
        grid=(nj // jb,),
        in_specs=[whole] * 7 + [pl.BlockSpec((ni, jb, pairs), lambda g: (0, g, 0))],
        out_specs=[
            pl.BlockSpec((ni, jb, pairs), lambda g: (0, g, 0)),
            fixed(rows.shape),
            fixed(cols.shape),
            fixed((cc + 8, pairs)),
        ],
        out_shape=[
            jax.ShapeDtypeStruct((ni, nj, pairs), BF16),
            jax.ShapeDtypeStruct(rows.shape, BF16),
            jax.ShapeDtypeStruct(cols.shape, BF16),
            jax.ShapeDtypeStruct((cc + 8, pairs), F32),
        ],
        scratch_shapes=[
            pltpu.VMEM((2, SEQS, CH * LANES), BF16),
            pltpu.VMEM((2, CH * LANES, SEQS), BF16),
            pltpu.VMEM((2, nj * CH, SEQS), BF16),
            pltpu.VMEM((ni * CH, SEQS), F32),
            pltpu.VMEM((cc, jb * LANES), BF16),
            pltpu.VMEM((jb * CH, CH * LANES), BF16),
            pltpu.VMEM((pairs, jb * LANES), BF16),
            pltpu.VMEM((pairs, jb * LANES), F32),
            pltpu.VMEM((ni * jb, pairs), F32),
            pltpu.VMEM((pairs, jb * LANES), F32),
            pltpu.VMEM((2, SEQS, CH * LANES), F32),
            pltpu.VMEM((cc, pairs), F32),
            pltpu.VMEM((2, nj * CH, SEQS), BF16),
            pltpu.VMEM((SEQS, jb * CH), BF16),
        ],
        compiler_params=pltpu.CompilerParams(
            dimension_semantics=("arbitrary",), vmem_limit_bytes=50 * 1024 * 1024
        ),
    )(rows, cols, weight, mirrored, weight.T, mirrored.T, bias.reshape(pairs, 1), upstream)


def local(left_features, right_features, weight, bias, upstream):
    row_count = lax.axis_size("row")
    col_count = lax.axis_size("col")
    ratio = col_count // row_count
    col_index = lax.axis_index("col")
    own = left_features.shape[0]
    portion = col_index % ratio
    owner = col_index // ratio
    mine = jnp.stack([left_features, right_features]).reshape(2, own, SEQS, CH)
    mine = mine.transpose(0, 1, 3, 2).reshape(2, own * CH, SEQS)
    rows = lax.all_gather(mine, "col", axis=0)
    piece = lax.dynamic_slice_in_dim(rows, portion * row_count, row_count, 0)
    recv = lax.all_to_all(piece, "row", split_axis=0, concat_axis=0, tiled=True)
    part = lax.dynamic_index_in_dim(recv, owner, 0, keepdims=False)
    cols = lax.all_gather(part, "row", axis=0)
    pair_out, d_rows, d_cols, d_weight = tile(rows, cols, weight, bias, upstream)
    total = lax.psum(d_weight, ("row", "col"))
    from_col = lax.all_to_all(d_cols, "row", split_axis=0, concat_axis=0, tiled=True)
    col_sum = jnp.sum(from_col.astype(F32), axis=0).astype(BF16)
    moves = [
        (r * col_count + q, q * row_count + r) for r in range(row_count) for q in range(col_count)
    ]
    col_sum = lax.ppermute(col_sum, ("row", "col"), moves)
    from_row = lax.all_to_all(d_rows, "col", split_axis=0, concat_axis=0, tiled=True)
    grads = jnp.sum(from_row.astype(F32), axis=0) + col_sum.astype(F32)
    grads = grads.astype(BF16).reshape(2, own, CH, SEQS).transpose(0, 1, 3, 2)
    grads = grads.reshape(2, own, SEQS * CH)
    cc = CH * CH
    return pair_out, grads[0], grads[1], total[:cc], total[cc]


def solution(mesh):
    placed = (P(("row", "col"), None), P(("row", "col"), None), P(), P(), P("row", "col", None))
    return jax.shard_map(
        local,
        mesh=mesh,
        in_specs=placed,
        out_specs=(
            P("row", "col", None),
            P(("row", "col"), None),
            P(("row", "col"), None),
            P(),
            P(),
        ),
        check_vma=False,
    )
```

time: 877 us -> 354 us (0.40)
  local copies, waits for them, and re-layouts: 365 us -> 11 us
  matrix products: 216 us -> 0 us
  blocking collectives: 149 us -> 22.6 us
  Pallas kernels: 0 us -> 115 us
  waiting for transfers between devices: 90.9 us -> 181 us
  loops' own time: 10.2 us -> 0 us
    dot_general x72 -> x0, matrix products: 216 us -> none  [the longest x12 73.9 us: one_block(): jnp.einsum(col_form, d_outer, rows, preferred_element_type=jnp.float32)]
    convert_element_type x38 -> x0, local copies, waits for them, and re-layouts: 164 us -> none  [the longest x24 142 us: one_block(): outer = outer.reshape(block_rows * across, CH * CH).astype(jnp.bfloat16)]
    pallas_call x0 -> x1, Pallas kernels: none -> 115 us  [tile(): pl.pallas_call(functools.partial(tile_kernel, jb, ni, nj), grid=(nj // jb...]
    reshape x28 -> x2, local copies, waits for them, and re-layouts: 87.1 us -> 0.26 us  [the longest x1 0.14 us: tile(): weight.reshape(CH, CH, pairs).transpose(1, 0, 2).reshape(cc, pairs)]
    psum x2 -> x1, waiting for transfers between devices: 88.5 us -> 142 us  [local(): total = lax.psum(d_weight, ('row', 'col'))]
    unnamed x1 -> x0, blocking collectives: 49.7 us -> none
    all_gather x4 -> x1, blocking collectives: 59.8 us -> 11.6 us  [local(): cols = lax.all_gather(part, 'row', axis=0)]
    psum x1 -> x0, blocking collectives: 40 us -> none  [local(): lax.psum((weight_one + weight_two, bias_one + bias_two), ('row', 'col'))]
  transfers between devices with their start and end apart: 8 -> 5, of which waited for: 3 -> 3; matrix products, arithmetic and copies ran while one was open for 40% -> 1% of each run, Pallas kernels for 0% -> 0%
where the time goes in v1:
time: 354 us; the launch traced here: 353 us
  waiting for transfers between devices  181 us (51%)
  Pallas kernels  115 us (32%)
  blocking collectives  22.6 us (6%)
  between operations  14.2 us (4%)
  local copies, waits for them, and re-layouts  11 us (3%)
  starting transfers between devices  7.98 us (2%)
    psum x1, waiting for transfers between devices, local(): total = lax.psum(d_weight, ('row', 'col'))  142 us
    pallas_call x1, Pallas kernels, tile(): pl.pallas_call(functools.partial(tile_kernel, jb, ni, nj), grid=(nj // jb...  115 us
    all_gather x1, waiting for transfers between devices, local(): rows = lax.all_gather(mine, 'col', axis=0)  27.9 us
    all_gather x1, blocking collectives, local(): cols = lax.all_gather(part, 'row', axis=0)  11.6 us
    all_to_all x1, blocking collectives, local(): lax.all_to_all(d_cols, 'row', split_axis=0, concat_axis=0, tiled=True)  11.1 us
    all_to_all x1, waiting for transfers between devices, local(): recv = lax.all_to_all(piece, 'row', split_axis=0, concat_axis=0, tiled=True)  10.8 us
  transfers between devices with their start and end apart: 5, of which 3 were waited for; matrix products, arithmetic and copies ran while one was open for 1% of the time, Pallas kernels for 0%

profile of v1, /device:TPU:0, one launch (start us, length us, event | category | flops | bytes accessed | tf_op | source)
XLA Modules:
  0.0 353.1 jit_solution(11628672938791954764)
XLA Ops:
  7.2 0.0 all-gather.2.cloned.1.call-start
  7.2 1.2 stack.9
  8.4 0.2 copy.29
  8.6 1.2 stack.10
  9.8 0.2 copy.30
  10.0 0.7 pad_maximum_fusion
  10.7 0.0 all-gather.2.cloned.1.call-update
  10.7 0.0 copy-start.1
  10.7 0.0 copy-start
  10.7 27.9 %all-gather.2.cloned.1.call-done.rows_ref = bf16[8,2,384,128]{3,2,1,0:T(8,128)(2,1)} async-done(((bf16[1,2,384,128]{3,2,1,0:T(8,128)(2,1)}), bf16[8,2,384,128]{3,2,1,0:T(8,128)(2,1)}) %all-gather.2.cloned.1.call-update) | async-done | bytes 1572880 | tf_op jit(solution)/shard_map/all_gather | solution.py:220
  38.6 2.1 constant_dynamic-slice_fusion.1
  40.7 3.6 %all-to-all-start = ((bf16[4,2,384,128]{3,2,1,0:T(8,128)(2,1)}), bf16[4,2,384,128]{3,2,1,0:T(8,128)(2,1)S(1)}, u32[]{:S(2)}, u32[]{:S(2)}) async-start(bf16[4,2,384,128]{3,2,1,0:T(8,128)(2,1)} %constant_dynamic-slice_fusion.1), calls=%async_computation | async-start | bytes 1572864 | tf_op jit(solution)/shard_map/all_to_all | solution.py:222
  44.3 0.0 copy-done.1
  44.3 0.1 copy.34.bias_ref
  44.4 0.0 copy-done
  44.5 0.1 copy.32
  44.6 0.1 copy.31
  44.7 0.1 copy.33
  44.9 10.8 %all-to-all-done = bf16[4,2,384,128]{3,2,1,0:T(8,128)(2,1)S(1)} async-done(((bf16[4,2,384,128]{3,2,1,0:T(8,128)(2,1)}), bf16[4,2,384,128]{3,2,1,0:T(8,128)(2,1)S(1)}, u32[]{:S(2)}, u32[]{:S(2)}) %all-to-all-start) | async-done | bytes 786464 | tf_op jit(solution)/shard_map/all_to_all | solution.py:222
  55.7 11.6 %all_gather.8.cols_ref = bf16[4,2,384,128]{3,2,1,0:T(8,128)(2,1)S(1)} all-gather(bf16[1,2,384,128]{3,2,1,0:T(8,128)(2,1)S(1)} %constant_dynamic-slice_fusion), channel_id=1, replica_groups=mesh['row'=4,'col'=8] {'row'}, dimensions={0}, use_global_device_ids=true | all-gather | bytes 983040 | tf_op jit(solution)/shard_map/all_gather | solution.py:224
  67.3 115.0 %shard_map.92 = (bf16[96,48,128]{2,1,0:T(8,128)(2,1)}, bf16[8,2,384,128]{3,2,1,0:T(8,128)(2,1)}, bf16[4,2,384,128]{3,2,1,0:T(8,128)(2,1)S(1)}, f32[1032,128]{1,0:T(8,128)}) custom-call(bf16[8,2,384,128]{3,2,1,0:T(8,128)(2,1)} %all-gather.2.cloned.1.call-done.rows_ref, bf16[4,2,384,128]{3,2,1,0:T(8,128)(2,1)S(1)} %all_gather.8.cols_ref, ...), custom_call_target="tpu_custom_call" | custom-call | tf_op jit(solution)/shard_map/pallas_call | solution.py:172
  182.3 11.1 %all_to_all.15 = bf16[4,2,384,128]{3,2,1,0:T(8,128)(2,1)S(1)} all-to-all(bf16[4,2,384,128]{3,2,1,0:T(8,128)(2,1)S(1)} %get-tuple-element.11), channel_id=1, replica_groups=mesh['row'=4,'col'=8] {'row'}, dimensions={0} | all-to-all | bytes 1572864 | tf_op jit(solution)/shard_map/all_to_all | solution.py:227
  193.4 3.6 %all-to-all-start.1 = ((bf16[8,2,384,128]{3,2,1,0:T(8,128)(2,1)}), bf16[8,2,384,128]{3,2,1,0:T(8,128)(2,1)S(1)}, u32[]{:S(2)}, u32[]{:S(2)}) async-start(bf16[8,2,384,128]{3,2,1,0:T(8,128)(2,1)} %get-tuple-element.10), calls=%async_computation.1 | async-start | bytes 3145728 | tf_op jit(solution)/shard_map/all_to_all | solution.py:233
  197.0 0.0 all-reduce.2.cloned.1.call-start
  197.0 0.7 all-reduce.2.cloned.1.call-update
  197.7 0.2 reduce_sum.22
  197.9 0.7 collective-permute-start
  198.6 141.7 %all-reduce.2.cloned.1.call-done = f32[1032,128]{1,0:T(8,128)} async-done(((f32[1032,128]{1,0:T(8,128)}), f32[1032,128]{1,0:T(8,128)}) %all-reduce.2.cloned.1.call-update) | async-done | bytes 528400 | tf_op jit(solution)/shard_map/psum | solution.py:226
  340.3 1.2 slice_bitcast_fusion
  341.5 1.9 slice.20
  343.4 0.0 all-to-all-done.1
  343.4 0.2 convert_reduce_fusion
  343.6 0.0 collective-permute-done
  343.6 0.1 add_convert_fusion
  343.7 0.2 copy.36
  343.9 1.1 squeeze.12
  345.0 0.2 copy.35
  345.2 1.1 squeeze.11
  (2 shorter events, 0.0 us)
Async XLA Ops:
  7.2 31.4 %all-gather.2.cloned.1.call-start = ((), (), s32[]{:S(2)}) async-start(), calls=%async_computation.3 | async-start | bytes 1769472 | tf_op jit(solution)/shard_map/all_gather | solution.py:220
  10.7 33.6 %copy-start.1 = (f32[128]{0:T(128)S(1)}, f32[128]{0:T(128)}, u32[]{:S(2)}) copy-start(f32[128]{0:T(128)} %param.8) | copy-start | bytes 1540
  10.7 33.7 %copy-start = (bf16[1024,128]{1,0:T(8,128)(2,1)S(1)}, bf16[1024,128]{1,0:T(8,128)(2,1)}, u32[]{:S(2)}) copy-start(bf16[1024,128]{1,0:T(8,128)(2,1)} %wd_ref.1) | copy-start | bytes 786436
  40.7 15.0 %all-to-all-start = ((bf16[4,2,384,128]{3,2,1,0:T(8,128)(2,1)}), bf16[4,2,384,128]{3,2,1,0:T(8,128)(2,1)S(1)}, u32[]{:S(2)}, u32[]{:S(2)}) async-start(bf16[4,2,384,128]{3,2,1,0:T(8,128)(2,1)} %constant_dynamic-slice_fusion.1), calls=%async_computation | async-start | bytes 1572864 | tf_op jit(solution)/shard_map/all_to_all | solution.py:222
  193.4 150.0 %all-to-all-start.1 = ((bf16[8,2,384,128]{3,2,1,0:T(8,128)(2,1)}), bf16[8,2,384,128]{3,2,1,0:T(8,128)(2,1)S(1)}, u32[]{:S(2)}, u32[]{:S(2)}) async-start(bf16[8,2,384,128]{3,2,1,0:T(8,128)(2,1)} %get-tuple-element.10), calls=%async_computation.1 | async-start | bytes 3145728 | tf_op jit(solution)/shard_map/all_to_all | solution.py:233
  197.0 143.4 %all-reduce.2.cloned.1.call-start = ((), (), s32[]{:S(2)}) async-start(), calls=%async_computation.4 | async-start | bytes 1056768 | tf_op jit(solution)/shard_map/psum | solution.py:226
  197.9 145.7 %collective-permute-start = (bf16[2,384,128]{2,1,0:T(8,128)(2,1)S(1)}, bf16[2,384,128]{2,1,0:T(8,128)(2,1)S(1)}, u32[]{:S(2)}, u32[]{:S(2)}) collective-permute-start(bf16[2,384,128]{2,1,0:T(8,128)(2,1)S(1)} %reduce_sum.22), channel_id=1, source_target_pairs={{0,0},{1,4},{2,8},{3,12},{4,16},{5,20},{6,24},{7,28},{8,1},{9,5},{... | collective-permute-start | bytes 589832 | tf_op jit(solution)/shard_map/ppermute | solution.py:232
Sparse Core Ops, SparseCore 0:
  10.8 27.7 all-gather.1
  203.0 137.2 all-reduce.1

commit v2 on v1

--- a/solution.py
+++ b/solution.py
@@ -223,19 +223,42 @@
     part = lax.dynamic_index_in_dim(recv, owner, 0, keepdims=False)
     cols = lax.all_gather(part, "row", axis=0)
     pair_out, d_rows, d_cols, d_weight = tile(rows, cols, weight, bias, upstream)
-    total = lax.psum(d_weight, ("row", "col"))
-    from_col = lax.all_to_all(d_cols, "row", split_axis=0, concat_axis=0, tiled=True)
-    col_sum = jnp.sum(from_col.astype(F32), axis=0).astype(BF16)
+    cc, pairs = weight.shape
+    joint = d_weight.astype(BF16)
+    send = jnp.concatenate(
+        [
+            d_rows.reshape(col_count, 2 * own * CH, SEQS),
+            joint[:cc].reshape(col_count, cc // col_count, pairs),
+            jnp.broadcast_to(joint[cc:][None], (col_count, 8, pairs)),
+        ],
+        axis=1,
+    )
+    from_row = lax.all_to_all(send, "col", split_axis=0, concat_axis=0, tiled=True)
+    row_sum = jnp.sum(from_row.astype(F32), axis=0)
+    size = 2 * own * CH
+    joint = row_sum[size:].astype(BF16)
+    deep = cc // col_count
+    send = jnp.concatenate(
+        [
+            d_cols.reshape(row_count, size, SEQS),
+            joint[:deep].reshape(row_count, deep // row_count, pairs),
+            jnp.broadcast_to(joint[deep:][None], (row_count, 8, pairs)),
+        ],
+        axis=1,
+    )
+    from_col = lax.all_to_all(send, "row", split_axis=0, concat_axis=0, tiled=True)
+    col_sum = jnp.sum(from_col.astype(F32), axis=0)
+    chunk = col_sum[size : size + deep // row_count]
+    grad_bias = col_sum[size + deep // row_count]
+    grad_weight = lax.all_gather(chunk, ("col", "row"), axis=0, tiled=True)
     moves = [
         (r * col_count + q, q * row_count + r) for r in range(row_count) for q in range(col_count)
     ]
-    col_sum = lax.ppermute(col_sum, ("row", "col"), moves)
-    from_row = lax.all_to_all(d_rows, "col", split_axis=0, concat_axis=0, tiled=True)
-    grads = jnp.sum(from_row.astype(F32), axis=0) + col_sum.astype(F32)
+    col_sum = lax.ppermute(col_sum[:size].astype(BF16), ("row", "col"), moves)
+    grads = row_sum[:size] + col_sum.astype(F32)
     grads = grads.astype(BF16).reshape(2, own, CH, SEQS).transpose(0, 1, 3, 2)
     grads = grads.reshape(2, own, SEQS * CH)
-    cc = CH * CH
-    return pair_out, grads[0], grads[1], total[:cc], total[cc]
+    return pair_out, grads[0], grads[1], grad_weight, grad_bias
 
 
 def solution(mesh):

time: 354 us -> 326 us (0.921)
  waiting for transfers between devices: 181 us -> 38.7 us
  blocking collectives: 22.6 us -> 142 us
  starting transfers between devices: 7.98 us -> 4.36 us
    psum x1 -> x0, waiting for transfers between devices: 142 us -> none  [local(): total = lax.psum(d_weight, ('row', 'col'))]
    all_gather x0 -> x1, blocking collectives: none -> 68.3 us  [local(): grad_weight = lax.all_gather(chunk, ('col', 'row'), axis=0, tiled=True)]
    all_to_all x1 -> x2, blocking collectives: 11.1 us -> 61.7 us  [the longest x1 46.8 us: local(): lax.all_to_all(send, 'col', split_axis=0, concat_axis=0, tiled=True)]
    all_to_all x1 -> x0, starting transfers between devices: 3.58 us -> none  [local(): lax.all_to_all(d_rows, 'col', split_axis=0, concat_axis=0, tiled=True)]
  transfers between devices with their start and end apart: 5 -> 3, of which waited for: 3 -> 2; matrix products, arithmetic and copies ran while one was open for 1% -> 0% of each run, Pallas kernels for 0% -> 0%
where the time goes in v2:
time: 326 us
  blocking collectives  142 us (44%)
  Pallas kernels  115 us (35%)
  waiting for transfers between devices  38.7 us (12%)
  between operations  14.2 us (4%)
  local copies, waits for them, and re-layouts  9.33 us (3%)
  starting transfers between devices  4.36 us (1%)
    pallas_call x1, Pallas kernels, tile(): pl.pallas_call(functools.partial(tile_kernel, jb, ni, nj), grid=(nj // jb...  115 us
    all_gather x1, blocking collectives, local(): grad_weight = lax.all_gather(chunk, ('col', 'row'), axis=0, tiled=True)  68.3 us
    all_to_all x1, blocking collectives, local(): lax.all_to_all(send, 'col', split_axis=0, concat_axis=0, tiled=True)  46.8 us
    all_gather x1, waiting for transfers between devices, local(): rows = lax.all_gather(mine, 'col', axis=0)  27.9 us
    all_to_all x1, blocking collectives, local(): lax.all_to_all(send, 'row', split_axis=0, concat_axis=0, tiled=True)  14.9 us
    all_gather x1, blocking collectives, local(): cols = lax.all_gather(part, 'row', axis=0)  11.6 us
    all_to_all x1, waiting for transfers between devices, local(): recv = lax.all_to_all(piece, 'row', split_axis=0, concat_axis=0, tiled=True)  10.8 us
  transfers between devices with their start and end apart: 3, of which 2 were waited for; matrix products, arithmetic and copies ran while one was open for 0% of the time, Pallas kernels for 0%

profile of v2, /device:TPU:0, one launch (start us, length us, event | category | flops | bytes accessed | tf_op | source)
XLA Modules:
  0.0 325.7 jit_solution(7766472362756977615)
XLA Ops:
  7.2 0.0 all-gather.2.cloned.1.call-start
  7.2 1.2 stack.9
  8.4 0.2 copy.29
  8.6 1.2 stack.10
  9.8 0.2 copy.30
  10.0 0.0 copy-start.1
  10.0 0.0 copy-start
  10.0 0.7 pad_maximum_fusion.2
  10.7 0.0 all-gather.2.cloned.1.call-update
  10.7 27.9 %all-gather.2.cloned.1.call-done.rows_ref = bf16[8,2,384,128]{3,2,1,0:T(8,128)(2,1)} async-done(((bf16[1,2,384,128]{3,2,1,0:T(8,128)(2,1)}), bf16[8,2,384,128]{3,2,1,0:T(8,128)(2,1)}) %all-gather.2.cloned.1.call-update) | async-done | bytes 1572880 | tf_op jit(solution)/shard_map/all_gather | solution.py:220
  38.6 2.1 constant_dynamic-slice_fusion.1
  40.7 3.6 %all-to-all-start = ((bf16[4,2,384,128]{3,2,1,0:T(8,128)(2,1)}), bf16[4,2,384,128]{3,2,1,0:T(8,128)(2,1)S(1)}, u32[]{:S(2)}, u32[]{:S(2)}) async-start(bf16[4,2,384,128]{3,2,1,0:T(8,128)(2,1)} %constant_dynamic-slice_fusion.1), calls=%async_computation | async-start | bytes 1572864 | tf_op jit(solution)/shard_map/all_to_all | solution.py:222
  44.4 0.0 copy-done.1
  44.4 0.1 copy.34.bias_ref
  44.5 0.0 copy-done
  44.5 0.1 copy.32
  44.6 0.1 copy.31
  44.7 0.1 copy.33
  44.9 10.8 %all-to-all-done = bf16[4,2,384,128]{3,2,1,0:T(8,128)(2,1)S(1)} async-done(((bf16[4,2,384,128]{3,2,1,0:T(8,128)(2,1)}), bf16[4,2,384,128]{3,2,1,0:T(8,128)(2,1)S(1)}, u32[]{:S(2)}, u32[]{:S(2)}) %all-to-all-start) | async-done | bytes 786464 | tf_op jit(solution)/shard_map/all_to_all | solution.py:222
  55.7 11.6 %all_gather.11.cols_ref = bf16[4,2,384,128]{3,2,1,0:T(8,128)(2,1)S(1)} all-gather(bf16[1,2,384,128]{3,2,1,0:T(8,128)(2,1)S(1)} %constant_dynamic-slice_fusion), channel_id=1, replica_groups=mesh['row'=4,'col'=8] {'row'}, dimensions={0}, use_global_device_ids=true | all-gather | bytes 983040 | tf_op jit(solution)/shard_map/all_gather | solution.py:224
  67.3 114.7 %shard_map.92 = (bf16[96,48,128]{2,1,0:T(8,128)(2,1)}, bf16[8,2,384,128]{3,2,1,0:T(8,128)(2,1)}, bf16[4,2,384,128]{3,2,1,0:T(8,128)(2,1)S(1)}, f32[1032,128]{1,0:T(8,128)S(1)}) custom-call(bf16[8,2,384,128]{3,2,1,0:T(8,128)(2,1)} %all-gather.2.cloned.1.call-done.rows_ref, bf16[4,2,384,128]{3,2,1,0:T(8,128)(2,1)S(1)} %all_gather.11.cols_ref, ...), custom_call_target="tpu_custom_call" | custom-call | tf_op jit(solution)/shard_map/pallas_call | solution.py:172
  182.1 1.5 pad_maximum_fusion
  183.6 46.8 %all_to_all.15 = bf16[8,904,128]{2,1,0:T(8,128)(2,1)S(1)} all-to-all(bf16[8,904,128]{2,1,0:T(8,128)(2,1)S(1)} %pad_maximum_fusion), channel_id=1, replica_groups=mesh['row'=4,'col'=8] {'col'}, dimensions={0} | all-to-all | bytes 3702784 | tf_op jit(solution)/shard_map/all_to_all | solution.py:236
  230.4 0.3 convert_reduce_fusion
  230.8 0.1 pad_maximum_fusion.1
  230.8 14.9 %all_to_all.16 = bf16[4,808,128]{2,1,0:T(8,128)(2,1)S(1)} all-to-all(bf16[4,808,128]{2,1,0:T(8,128)(2,1)S(1)} %pad_maximum_fusion.1), channel_id=1, replica_groups=mesh['row'=4,'col'=8] {'row'}, dimensions={0} | all-to-all | bytes 1654784 | tf_op jit(solution)/shard_map/all_to_all | solution.py:249
  245.7 0.1 convert_reduce_fusion.1
  245.9 0.7 collective-permute-start
  246.6 68.3 %all_gather.12 = f32[1024,128]{1,0:T(8,128)S(1)} all-gather(f32[32,128]{1,0:T(8,128)S(1)} %slice.55), channel_id=1, replica_groups=mesh['row'=4,'col'=8] {'col','row'}, dimensions={0}, use_global_device_ids=true | all-gather | bytes 540672 | tf_op jit(solution)/shard_map/all_gather | solution.py:253
  314.8 0.5 slice_bitcast_fusion
  315.4 0.0 collective-permute-done
  315.4 0.4 copy.35
  315.8 0.1 fusion.1
  315.9 1.1 squeeze.12
  317.0 1.1 squeeze.11
  318.0 0.8 copy.37
  (12 shorter events, 0.2 us)
Async XLA Ops:
  7.2 31.5 %all-gather.2.cloned.1.call-start = ((), (), s32[]{:S(2)}) async-start(), calls=%async_computation.3 | async-start | bytes 1769472 | tf_op jit(solution)/shard_map/all_gather | solution.py:220
  10.0 34.4 %copy-start.1 = (f32[128]{0:T(128)S(1)}, f32[128]{0:T(128)}, u32[]{:S(2)}) copy-start(f32[128]{0:T(128)} %param.8) | copy-start | bytes 1540
  10.0 34.5 %copy-start = (bf16[1024,128]{1,0:T(8,128)(2,1)S(1)}, bf16[1024,128]{1,0:T(8,128)(2,1)}, u32[]{:S(2)}) copy-start(bf16[1024,128]{1,0:T(8,128)(2,1)} %wd_ref.1) | copy-start | bytes 786436
  40.7 15.0 %all-to-all-start = ((bf16[4,2,384,128]{3,2,1,0:T(8,128)(2,1)}), bf16[4,2,384,128]{3,2,1,0:T(8,128)(2,1)S(1)}, u32[]{:S(2)}, u32[]{:S(2)}) async-start(bf16[4,2,384,128]{3,2,1,0:T(8,128)(2,1)} %constant_dynamic-slice_fusion.1), calls=%async_computation | async-start | bytes 1572864 | tf_op jit(solution)/shard_map/all_to_all | solution.py:222
  245.9 69.5 %collective-permute-start = (bf16[768,128]{1,0:T(8,128)(2,1)S(1)}, bf16[768,128]{1,0:T(8,128)(2,1)S(1)}, u32[]{:S(2)}, u32[]{:S(2)}) collective-permute-start(bf16[768,128]{1,0:T(8,128)(2,1)S(1)} %slice.62), channel_id=1, source_target_pairs={{0,0},{1,4},{2,8},{3,12},{4,16},{5,20},{6,24},{7,28},{8,1},{9,5},{... | collective-permute-start | bytes 589832 | tf_op jit(solution)/shard_map/ppermute | solution.py:257
Sparse Core Ops, SparseCore 0:
  10.8 27.7 all-gather.1

commit v3 on v2

--- a/solution.py
+++ b/solution.py
@@ -250,7 +250,8 @@
     col_sum = jnp.sum(from_col.astype(F32), axis=0)
     chunk = col_sum[size : size + deep // row_count]
     grad_bias = col_sum[size + deep // row_count]
-    grad_weight = lax.all_gather(chunk, ("col", "row"), axis=0, tiled=True)
+    grad_weight = lax.all_gather(chunk, "row", axis=0, tiled=True)
+    grad_weight = lax.all_gather(grad_weight, "col", axis=0, tiled=True)
     moves = [
         (r * col_count + q, q * row_count + r) for r in range(row_count) for q in range(col_count)
     ]

time: 326 us -> 288 us (0.88)
  blocking collectives: 142 us -> 103 us
    all_gather x1 -> x2, blocking collectives: 68.3 us -> 29.9 us  [the longest x1 22.5 us: local(): grad_weight = lax.all_gather(grad_weight, 'col', axis=0, tiled=True)]
where the time goes in v3:
time: 288 us; the launch traced here: 287 us
  Pallas kernels  115 us (40%)
  blocking collectives  103 us (36%)
  waiting for transfers between devices  38.7 us (13%)
  between operations  14.2 us (5%)
  local copies, waits for them, and re-layouts  9.33 us (3%)
  starting transfers between devices  4.35 us (2%)
    pallas_call x1, Pallas kernels, tile(): pl.pallas_call(functools.partial(tile_kernel, jb, ni, nj), grid=(nj // jb...  115 us
    all_to_all x1, blocking collectives, local(): lax.all_to_all(send, 'col', split_axis=0, concat_axis=0, tiled=True)  46.8 us
    all_gather x1, waiting for transfers between devices, local(): rows = lax.all_gather(mine, 'col', axis=0)  27.9 us
    all_gather x1, blocking collectives, local(): grad_weight = lax.all_gather(grad_weight, 'col', axis=0, tiled=True)  22.5 us
    all_to_all x1, blocking collectives, local(): lax.all_to_all(send, 'row', split_axis=0, concat_axis=0, tiled=True)  14.9 us
    all_gather x1, blocking collectives, local(): cols = lax.all_gather(part, 'row', axis=0)  11.6 us
    all_to_all x1, waiting for transfers between devices, local(): recv = lax.all_to_all(piece, 'row', split_axis=0, concat_axis=0, tiled=True)  10.8 us
    all_gather x1, blocking collectives, local(): grad_weight = lax.all_gather(chunk, 'row', axis=0, tiled=True)  7.49 us
  transfers between devices with their start and end apart: 3, of which 2 were waited for; matrix products, arithmetic and copies ran while one was open for 0% of the time, Pallas kernels for 0%

profile of v3, /device:TPU:0, one launch (start us, length us, event | category | flops | bytes accessed | tf_op | source)
XLA Modules:
  0.0 287.3 jit_solution(3827297751144497131)
XLA Ops:
  7.2 0.0 all-gather.2.cloned.1.call-start
  7.2 1.2 stack.9
  8.4 0.2 copy.29
  8.6 1.2 stack.10
  9.8 0.2 copy.30
  10.0 0.0 copy-start.1
  10.0 0.0 copy-start
  10.0 0.7 pad_maximum_fusion.2
  10.7 0.0 all-gather.2.cloned.1.call-update
  10.7 27.9 %all-gather.2.cloned.1.call-done.rows_ref = bf16[8,2,384,128]{3,2,1,0:T(8,128)(2,1)} async-done(((bf16[1,2,384,128]{3,2,1,0:T(8,128)(2,1)}), bf16[8,2,384,128]{3,2,1,0:T(8,128)(2,1)}) %all-gather.2.cloned.1.call-update) | async-done | bytes 1572880 | tf_op jit(solution)/shard_map/all_gather | solution.py:220
  38.6 2.1 constant_dynamic-slice_fusion.1
  40.7 3.6 %all-to-all-start = ((bf16[4,2,384,128]{3,2,1,0:T(8,128)(2,1)}), bf16[4,2,384,128]{3,2,1,0:T(8,128)(2,1)S(1)}, u32[]{:S(2)}, u32[]{:S(2)}) async-start(bf16[4,2,384,128]{3,2,1,0:T(8,128)(2,1)} %constant_dynamic-slice_fusion.1), calls=%async_computation | async-start | bytes 1572864 | tf_op jit(solution)/shard_map/all_to_all | solution.py:222
  44.4 0.0 copy-done.1
  44.4 0.1 copy.34.bias_ref
  44.5 0.0 copy-done
  44.5 0.1 copy.32
  44.6 0.1 copy.31
  44.7 0.1 copy.33
  44.9 10.8 %all-to-all-done = bf16[4,2,384,128]{3,2,1,0:T(8,128)(2,1)S(1)} async-done(((bf16[4,2,384,128]{3,2,1,0:T(8,128)(2,1)}), bf16[4,2,384,128]{3,2,1,0:T(8,128)(2,1)S(1)}, u32[]{:S(2)}, u32[]{:S(2)}) %all-to-all-start) | async-done | bytes 786464 | tf_op jit(solution)/shard_map/all_to_all | solution.py:222
  55.7 11.6 %all_gather.14.cols_ref = bf16[4,2,384,128]{3,2,1,0:T(8,128)(2,1)S(1)} all-gather(bf16[1,2,384,128]{3,2,1,0:T(8,128)(2,1)S(1)} %constant_dynamic-slice_fusion), channel_id=1, replica_groups=mesh['row'=4,'col'=8] {'row'}, dimensions={0}, use_global_device_ids=true | all-gather | bytes 983040 | tf_op jit(solution)/shard_map/all_gather | solution.py:224
  67.3 114.7 %shard_map.92 = (bf16[96,48,128]{2,1,0:T(8,128)(2,1)}, bf16[8,2,384,128]{3,2,1,0:T(8,128)(2,1)}, bf16[4,2,384,128]{3,2,1,0:T(8,128)(2,1)S(1)}, f32[1032,128]{1,0:T(8,128)S(1)}) custom-call(bf16[8,2,384,128]{3,2,1,0:T(8,128)(2,1)} %all-gather.2.cloned.1.call-done.rows_ref, bf16[4,2,384,128]{3,2,1,0:T(8,128)(2,1)S(1)} %all_gather.14.cols_ref, ...), custom_call_target="tpu_custom_call" | custom-call | tf_op jit(solution)/shard_map/pallas_call | solution.py:172
  182.1 1.5 pad_maximum_fusion
  183.6 46.8 %all_to_all.15 = bf16[8,904,128]{2,1,0:T(8,128)(2,1)S(1)} all-to-all(bf16[8,904,128]{2,1,0:T(8,128)(2,1)S(1)} %pad_maximum_fusion), channel_id=1, replica_groups=mesh['row'=4,'col'=8] {'col'}, dimensions={0} | all-to-all | bytes 3702784 | tf_op jit(solution)/shard_map/all_to_all | solution.py:236
  230.4 0.3 convert_reduce_fusion
  230.8 0.1 pad_maximum_fusion.1
  230.8 14.9 %all_to_all.16 = bf16[4,808,128]{2,1,0:T(8,128)(2,1)S(1)} all-to-all(bf16[4,808,128]{2,1,0:T(8,128)(2,1)S(1)} %pad_maximum_fusion.1), channel_id=1, replica_groups=mesh['row'=4,'col'=8] {'row'}, dimensions={0} | all-to-all | bytes 1654784 | tf_op jit(solution)/shard_map/all_to_all | solution.py:249
  245.7 0.1 convert_reduce_fusion.1
  245.9 7.5 %all_gather.15 = f32[128,128]{1,0:T(8,128)S(1)} all-gather(f32[32,128]{1,0:T(8,128)S(1)} %slice.55), channel_id=1, replica_groups=mesh['row'=4,'col'=8] {'row'}, dimensions={0}, use_global_device_ids=true | all-gather | bytes 81920 | tf_op jit(solution)/shard_map/all_gather | solution.py:253
  253.4 0.7 collective-permute-start
  254.0 22.5 %all_gather.16 = f32[1024,128]{1,0:T(8,128)S(1)} all-gather(f32[128,128]{1,0:T(8,128)S(1)} %all_gather.15), channel_id=1, replica_groups=mesh['row'=4,'col'=8] {'col'}, dimensions={0}, use_global_device_ids=true | all-gather | bytes 589824 | tf_op jit(solution)/shard_map/all_gather | solution.py:254
  276.5 0.5 slice_bitcast_fusion
  277.0 0.0 collective-permute-done
  277.0 0.4 copy.35
  277.4 0.1 fusion.1
  277.5 1.1 squeeze.12
  278.6 1.1 squeeze.11
  279.7 0.8 copy.37
  (12 shorter events, 0.2 us)
Async XLA Ops:
  7.2 31.5 %all-gather.2.cloned.1.call-start = ((), (), s32[]{:S(2)}) async-start(), calls=%async_computation.3 | async-start | bytes 1769472 | tf_op jit(solution)/shard_map/all_gather | solution.py:220
  10.0 34.4 %copy-start.1 = (f32[128]{0:T(128)S(1)}, f32[128]{0:T(128)}, u32[]{:S(2)}) copy-start(f32[128]{0:T(128)} %param.8) | copy-start | bytes 1540
  10.0 34.5 %copy-start = (bf16[1024,128]{1,0:T(8,128)(2,1)S(1)}, bf16[1024,128]{1,0:T(8,128)(2,1)}, u32[]{:S(2)}) copy-start(bf16[1024,128]{1,0:T(8,128)(2,1)} %wd_ref.1) | copy-start | bytes 786436
  40.7 15.0 %all-to-all-start = ((bf16[4,2,384,128]{3,2,1,0:T(8,128)(2,1)}), bf16[4,2,384,128]{3,2,1,0:T(8,128)(2,1)S(1)}, u32[]{:S(2)}, u32[]{:S(2)}) async-start(bf16[4,2,384,128]{3,2,1,0:T(8,128)(2,1)} %constant_dynamic-slice_fusion.1), calls=%async_computation | async-start | bytes 1572864 | tf_op jit(solution)/shard_map/all_to_all | solution.py:222
  253.4 23.6 %collective-permute-start = (bf16[768,128]{1,0:T(8,128)(2,1)S(1)}, bf16[768,128]{1,0:T(8,128)(2,1)S(1)}, u32[]{:S(2)}, u32[]{:S(2)}) collective-permute-start(bf16[768,128]{1,0:T(8,128)(2,1)S(1)} %slice.62), channel_id=1, source_target_pairs={{0,0},{1,4},{2,8},{3,12},{4,16},{5,20},{6,24},{7,28},{8,1},{9,5},{... | collective-permute-start | bytes 589832 | tf_op jit(solution)/shard_map/ppermute | solution.py:258
Sparse Core Ops, SparseCore 0:
  10.8 27.7 all-gather.1

commit v4 on v3

--- a/solution.py
+++ b/solution.py
@@ -227,16 +227,15 @@
     joint = d_weight.astype(BF16)
     send = jnp.concatenate(
         [
-            d_rows.reshape(col_count, 2 * own * CH, SEQS),
             joint[:cc].reshape(col_count, cc // col_count, pairs),
             jnp.broadcast_to(joint[cc:][None], (col_count, 8, pairs)),
         ],
         axis=1,
     )
-    from_row = lax.all_to_all(send, "col", split_axis=0, concat_axis=0, tiled=True)
-    row_sum = jnp.sum(from_row.astype(F32), axis=0)
     size = 2 * own * CH
-    joint = row_sum[size:].astype(BF16)
+    from_row = lax.all_to_all(d_rows, "col", split_axis=0, concat_axis=0, tiled=True)
+    shared = lax.all_to_all(send, "col", split_axis=0, concat_axis=0, tiled=True)
+    joint = jnp.sum(shared.astype(F32), axis=0).astype(BF16)
     deep = cc // col_count
     send = jnp.concatenate(
         [
@@ -256,7 +255,8 @@
         (r * col_count + q, q * row_count + r) for r in range(row_count) for q in range(col_count)
     ]
     col_sum = lax.ppermute(col_sum[:size].astype(BF16), ("row", "col"), moves)
-    grads = row_sum[:size] + col_sum.astype(F32)
+    row_sum = jnp.sum(from_row.astype(F32), axis=0).reshape(size, SEQS)
+    grads = row_sum + col_sum.astype(F32)
     grads = grads.astype(BF16).reshape(2, own, CH, SEQS).transpose(0, 1, 3, 2)
     grads = grads.reshape(2, own, SEQS * CH)
     return pair_out, grads[0], grads[1], grad_weight, grad_bias

time: 288 us -> 274 us (0.951)
  blocking collectives: 103 us -> 87 us
  starting transfers between devices: 4.35 us -> 7.94 us
    all_to_all x1, blocking collectives: 46.8 us -> 13.1 us  [local(): lax.all_to_all(send, 'col', split_axis=0, concat_axis=0, tiled=True)]
    all_gather x1, blocking collectives: 22.5 us -> 36.1 us  [local(): grad_weight = lax.all_gather(grad_weight, 'col', axis=0, tiled=True)]
    all_gather x1, blocking collectives: 7.49 us -> 11.3 us  [local(): grad_weight = lax.all_gather(chunk, 'row', axis=0, tiled=True)]
    all_to_all x0 -> x1, starting transfers between devices: none -> 3.58 us  [local(): lax.all_to_all(d_rows, 'col', split_axis=0, concat_axis=0, tiled=True)]
  transfers between devices with their start and end apart: 3 -> 4, of which waited for: 2 -> 2; matrix products, arithmetic and copies ran while one was open for 0% -> 1% of each run, Pallas kernels for 0% -> 0%
where the time goes in v4:
time: 274 us; the launch traced here: 273 us
  Pallas kernels  115 us (42%)
  blocking collectives  87 us (32%)
  waiting for transfers between devices  38.7 us (14%)
  between operations  14.3 us (5%)
  local copies, waits for them, and re-layouts  9.33 us (3%)
  starting transfers between devices  7.94 us (3%)
    pallas_call x1, Pallas kernels, tile(): pl.pallas_call(functools.partial(tile_kernel, jb, ni, nj), grid=(nj // jb...  115 us
    all_gather x1, blocking collectives, local(): grad_weight = lax.all_gather(grad_weight, 'col', axis=0, tiled=True)  36.1 us
    all_gather x1, waiting for transfers between devices, local(): rows = lax.all_gather(mine, 'col', axis=0)  27.9 us
    all_to_all x1, blocking collectives, local(): lax.all_to_all(send, 'row', split_axis=0, concat_axis=0, tiled=True)  14.9 us
    all_to_all x1, blocking collectives, local(): lax.all_to_all(send, 'col', split_axis=0, concat_axis=0, tiled=True)  13.1 us
    all_gather x1, blocking collectives, local(): cols = lax.all_gather(part, 'row', axis=0)  11.6 us
    all_gather x1, blocking collectives, local(): grad_weight = lax.all_gather(chunk, 'row', axis=0, tiled=True)  11.3 us
    all_to_all x1, waiting for transfers between devices, local(): recv = lax.all_to_all(piece, 'row', split_axis=0, concat_axis=0, tiled=True)  10.8 us
  transfers between devices with their start and end apart: 4, of which 2 were waited for; matrix products, arithmetic and copies ran while one was open for 1% of the time, Pallas kernels for 0%

profile of v4, /device:TPU:0, one launch (start us, length us, event | category | flops | bytes accessed | tf_op | source)
XLA Modules:
  0.0 273.2 jit_solution(6038715741781611089)
XLA Ops:
  7.2 0.0 all-gather.2.cloned.1.call-start
  7.2 1.2 stack.9
  8.4 0.2 copy.29
  8.6 1.2 stack.10
  9.8 0.2 copy.30
  10.0 0.7 pad_maximum_fusion.2
  10.7 0.0 all-gather.2.cloned.1.call-update
  10.7 0.0 copy-start.1
  10.7 0.0 copy-start
  10.7 27.9 %all-gather.2.cloned.1.call-done.rows_ref = bf16[8,2,384,128]{3,2,1,0:T(8,128)(2,1)} async-done(((bf16[1,2,384,128]{3,2,1,0:T(8,128)(2,1)}), bf16[8,2,384,128]{3,2,1,0:T(8,128)(2,1)}) %all-gather.2.cloned.1.call-update) | async-done | bytes 1572880 | tf_op jit(solution)/shard_map/all_gather | solution.py:220
  38.6 2.1 constant_dynamic-slice_fusion.1
  40.7 3.6 %all-to-all-start = ((bf16[4,2,384,128]{3,2,1,0:T(8,128)(2,1)}), bf16[4,2,384,128]{3,2,1,0:T(8,128)(2,1)S(1)}, u32[]{:S(2)}, u32[]{:S(2)}) async-start(bf16[4,2,384,128]{3,2,1,0:T(8,128)(2,1)} %constant_dynamic-slice_fusion.1), calls=%async_computation | async-start | bytes 1572864 | tf_op jit(solution)/shard_map/all_to_all | solution.py:222
  44.3 0.0 copy-done.1
  44.3 0.1 copy.34.bias_ref
  44.4 0.0 copy-done
  44.5 0.1 copy.32
  44.6 0.1 copy.31
  44.7 0.1 copy.33
  44.9 10.8 %all-to-all-done = bf16[4,2,384,128]{3,2,1,0:T(8,128)(2,1)S(1)} async-done(((bf16[4,2,384,128]{3,2,1,0:T(8,128)(2,1)}), bf16[4,2,384,128]{3,2,1,0:T(8,128)(2,1)S(1)}, u32[]{:S(2)}, u32[]{:S(2)}) %all-to-all-start) | async-done | bytes 786464 | tf_op jit(solution)/shard_map/all_to_all | solution.py:222
  55.7 11.6 %all_gather.14.cols_ref = bf16[4,2,384,128]{3,2,1,0:T(8,128)(2,1)S(1)} all-gather(bf16[1,2,384,128]{3,2,1,0:T(8,128)(2,1)S(1)} %constant_dynamic-slice_fusion), channel_id=1, replica_groups=mesh['row'=4,'col'=8] {'row'}, dimensions={0}, use_global_device_ids=true | all-gather | bytes 983040 | tf_op jit(solution)/shard_map/all_gather | solution.py:224
  67.3 114.7 %shard_map.92 = (bf16[96,48,128]{2,1,0:T(8,128)(2,1)}, bf16[8,2,384,128]{3,2,1,0:T(8,128)(2,1)}, bf16[4,2,384,128]{3,2,1,0:T(8,128)(2,1)S(1)}, f32[1032,128]{1,0:T(8,128)S(1)}) custom-call(bf16[8,2,384,128]{3,2,1,0:T(8,128)(2,1)} %all-gather.2.cloned.1.call-done.rows_ref, bf16[4,2,384,128]{3,2,1,0:T(8,128)(2,1)S(1)} %all_gather.14.cols_ref, ...), custom_call_target="tpu_custom_call" | custom-call | tf_op jit(solution)/shard_map/pallas_call | solution.py:172
  182.1 13.1 %all_to_all.20 = bf16[8,136,128]{2,1,0:T(8,128)(2,1)S(1)} all-to-all(bf16[8,136,128]{2,1,0:T(8,128)(2,1)S(1)} %pad_maximum_fusion.1), channel_id=1, replica_groups=mesh['row'=4,'col'=8] {'col'}, dimensions={0} | all-to-all | bytes 557056 | tf_op jit(solution)/shard_map/all_to_all | solution.py:237
  195.3 0.1 pad_maximum_fusion
  195.4 14.9 %all_to_all.21 = bf16[4,808,128]{2,1,0:T(8,128)(2,1)S(1)} all-to-all(bf16[4,808,128]{2,1,0:T(8,128)(2,1)S(1)} %pad_maximum_fusion), channel_id=1, replica_groups=mesh['row'=4,'col'=8] {'row'}, dimensions={0} | all-to-all | bytes 1654784 | tf_op jit(solution)/shard_map/all_to_all | solution.py:248
  210.2 3.6 %all-to-all-start.1 = ((bf16[8,2,384,128]{3,2,1,0:T(8,128)(2,1)}), bf16[8,2,384,128]{3,2,1,0:T(8,128)(2,1)S(1)}, u32[]{:S(2)}, u32[]{:S(2)}) async-start(bf16[8,2,384,128]{3,2,1,0:T(8,128)(2,1)} %get-tuple-element.10), calls=%async_computation.1 | async-start | bytes 3145728 | tf_op jit(solution)/shard_map/all_to_all | solution.py:236
  213.8 0.1 convert_reduce_fusion.1
  214.0 0.7 collective-permute-start
  214.7 11.3 %all_gather.15 = f32[128,128]{1,0:T(8,128)S(1)} all-gather(f32[32,128]{1,0:T(8,128)S(1)} %slice.46), channel_id=1, replica_groups=mesh['row'=4,'col'=8] {'row'}, dimensions={0}, use_global_device_ids=true | all-gather | bytes 81920 | tf_op jit(solution)/shard_map/all_gather | solution.py:252
  226.0 36.1 %all_gather.16 = f32[1024,128]{1,0:T(8,128)S(1)} all-gather(f32[128,128]{1,0:T(8,128)S(1)} %all_gather.15), channel_id=1, replica_groups=mesh['row'=4,'col'=8] {'col'}, dimensions={0}, use_global_device_ids=true | all-gather | bytes 589824 | tf_op jit(solution)/shard_map/all_gather | solution.py:253
  262.1 0.5 slice_bitcast_fusion
  262.6 0.0 all-to-all-done.1
  262.6 0.2 convert_reduce_fusion
  262.8 0.0 collective-permute-done
  262.9 0.4 copy.35
  263.3 0.1 fusion.1
  263.4 1.1 squeeze.12
  264.4 1.1 squeeze.11
  265.5 0.8 copy.37
  (13 shorter events, 0.2 us)
Async XLA Ops:
  7.2 31.4 %all-gather.2.cloned.1.call-start = ((), (), s32[]{:S(2)}) async-start(), calls=%async_computation.4 | async-start | bytes 1769472 | tf_op jit(solution)/shard_map/all_gather | solution.py:220
  10.7 33.6 %copy-start.1 = (f32[128]{0:T(128)S(1)}, f32[128]{0:T(128)}, u32[]{:S(2)}) copy-start(f32[128]{0:T(128)} %param.8) | copy-start | bytes 1540
  10.7 33.7 %copy-start = (bf16[1024,128]{1,0:T(8,128)(2,1)S(1)}, bf16[1024,128]{1,0:T(8,128)(2,1)}, u32[]{:S(2)}) copy-start(bf16[1024,128]{1,0:T(8,128)(2,1)} %wd_ref.1) | copy-start | bytes 786436
  40.7 15.0 %all-to-all-start = ((bf16[4,2,384,128]{3,2,1,0:T(8,128)(2,1)}), bf16[4,2,384,128]{3,2,1,0:T(8,128)(2,1)S(1)}, u32[]{:S(2)}, u32[]{:S(2)}) async-start(bf16[4,2,384,128]{3,2,1,0:T(8,128)(2,1)} %constant_dynamic-slice_fusion.1), calls=%async_computation | async-start | bytes 1572864 | tf_op jit(solution)/shard_map/all_to_all | solution.py:222
  210.2 52.4 %all-to-all-start.1 = ((bf16[8,2,384,128]{3,2,1,0:T(8,128)(2,1)}), bf16[8,2,384,128]{3,2,1,0:T(8,128)(2,1)S(1)}, u32[]{:S(2)}, u32[]{:S(2)}) async-start(bf16[8,2,384,128]{3,2,1,0:T(8,128)(2,1)} %get-tuple-element.10), calls=%async_computation.1 | async-start | bytes 3145728 | tf_op jit(solution)/shard_map/all_to_all | solution.py:236
  214.0 48.8 %collective-permute-start = (bf16[768,128]{1,0:T(8,128)(2,1)S(1)}, bf16[768,128]{1,0:T(8,128)(2,1)S(1)}, u32[]{:S(2)}, u32[]{:S(2)}) collective-permute-start(bf16[768,128]{1,0:T(8,128)(2,1)S(1)} %slice.50), channel_id=1, source_target_pairs={{0,0},{1,4},{2,8},{3,12},{4,16},{5,20},{6,24},{7,28},{8,1},{9,5},{... | collective-permute-start | bytes 589832 | tf_op jit(solution)/shard_map/ppermute | solution.py:257
Sparse Core Ops, SparseCore 0:
  10.8 27.7 all-gather.1
